TPU v7x, 256 devices: a whole 4x4x8 slice. The times are simulated.
256 devices in a mesh: wide: 64 (over y, x, z_hi, core), narrow: 4 (over z_lo).
Axes of the slice: x: 4, y: 4, z: 8 (z_hi: 2, z_lo: 4; z = z_hi * 4 + z_lo), core: 2. Of those that a mesh axis runs over, the one named last changes fastest.
Arguments:
- field: bfloat16 [64, 4, 1024, 1024], P('narrow', None, 'wide'), may hold values from -6 to 6
- spectral_weight: bfloat16 [64, 64, 64, 128], P('narrow', None, 'wide'), may hold values from -0.5 to 0.5
- cotangent: bfloat16 [64, 4, 1024, 1024], P('narrow', None, 'wide'), may hold values from -1.5 to 1.5
Outputs:
- output: bfloat16 [64, 4, 1024, 1024], P('narrow', None, 'wide')
- weight_grad: float32 [64, 64, 64, 128], P('narrow', None, 'wide')
- field_grad: bfloat16 [64, 4, 1024, 1024], P('narrow', None, 'wide')
All inputs are finite; a program needn't handle non-finite values.
Results may differ from a plain program's by a relative error of at most 0.012.
Values may be sent and summed in bfloat16 or wider, within the bound.
A program may use at most 64 MiB of HBM per device.

v0:
```python
import math

import jax
import jax.numpy as jnp
import ml_dtypes
import numpy as np
from jax import lax
from jax.experimental import pallas as pl
from jax.experimental.pallas import tpu as pltpu
from jax.sharding import PartitionSpec as P

X = 1024
Y = 1024
MX = 64
MY = 64
GROUP = 32
ROWS = 1024
MESH = pl.DeviceIdType.MESH
F32 = jnp.float32
BF16 = jnp.bfloat16


def mode_of(group, half):
    return (group // 2) * 4 + half * 2 + group % 2


def tables():
    step = np.float32(2.0 * math.pi / X)
    group = np.arange(GROUP)
    k = np.stack([mode_of(group, h) for h in range(2)], axis=1)
    ax = ((np.arange(X)[:, None, None] * k[None]) % X).astype(np.float32) * step
    fx = np.stack([np.cos(ax), -np.sin(ax)], axis=-1).reshape(X, 2 * MX)
    forward_x = (fx / np.float32(32)).astype(ml_dtypes.bfloat16)
    inverse_x = np.ascontiguousarray((fx / np.float32(4)).astype(ml_dtypes.bfloat16).T)
    m = np.arange(MY)
    q = np.where(m < MY // 2, m, m - MY + Y)
    ay = ((np.arange(Y)[:, None] * q[None]) % Y).astype(np.float32) * step
    cos, sin = np.cos(ay), np.sin(ay)
    fy = np.stack([np.concatenate([cos, -sin], 1), np.concatenate([sin, cos], 1)], 0)
    fy = (fy / np.float32(32)).astype(ml_dtypes.bfloat16)
    halves = []
    for h in range(2):
        y = 16 * mode_of(group, h)[:, None] + np.arange(16)[None]
        part = fy[:, y, :].reshape(2, GROUP, 2, 8, 2 * MY)
        halves.append(part.transpose(1, 0, 3, 2, 4).reshape(GROUP * 16, 4 * MY))
    return forward_x, inverse_x, np.stack(halves)


def halves_swapped(a):
    return pltpu.roll(a, MY, a.ndim - 1)


def low_lanes(shape):
    return lax.broadcasted_iota(jnp.int32, shape, len(shape) - 1) < MY


def exchange_kernel(
    field, cot, weight, fx_hbm, fy_hbm,
    back_out, grad_out, wg_out,
    rows_in, fx, fy, wt, w1, w2, xm, t32, send1, recv1, part, part_in, s_rows, a1, a2,
    mixpart, mix_in, cots, d1, d2, sg, modes, send2, recv2, wg,
    in_sem, s1_send, s1_recv, px_send, px_recv, rs_send, rs_recv, ag_send, ag_recv,
    mx_send, mx_recv, s2_send, s2_recv, wg_sem,
):
    w = lax.axis_index("wide")
    n = lax.axis_index("narrow")
    half = lax.rem(lax.div(w, 2), 2)
    g = lax.div(w, 4) * 2 + lax.rem(w, 2)
    partner = {"wide": w + 2 - 4 * half, "narrow": n}

    def member(i):
        other = lax.rem(g + i, GROUP)
        wide = lax.div(other, 2) * 4 + half * 2 + lax.rem(other, 2)
        return other, {"wide": wide, "narrow": n}

    def aside(i):
        other = lax.rem(n + i, 4)
        return other, {"wide": w, "narrow": other}

    chunk = ROWS // 4
    copies = []
    copies.append(pltpu.make_async_copy(fx_hbm, fx, in_sem.at[8]))
    for a, src in enumerate((field, cot)):
        for c in range(4):
            rows = pl.ds(c * chunk, chunk)
            copies.append(
                pltpu.make_async_copy(src.at[rows], rows_in.at[a, rows], in_sem.at[a * 4 + c])
            )
    fy_copy = pltpu.make_async_copy(fy_hbm.at[half], fy, in_sem.at[9])
    wt_copy = pltpu.make_async_copy(weight, wt, in_sem.at[10])
    for copy in copies:
        copy.start()
    fy_copy.start()
    wt_copy.start()

    barrier = pltpu.get_barrier_semaphore()

    def greet(i, _):
        pl.semaphore_signal(barrier, 1, device_id=member(i)[1], device_id_type=MESH)
        return 0

    lax.fori_loop(1, GROUP, greet, 0)
    pl.semaphore_signal(barrier, 1, device_id=partner, device_id_type=MESH)
    for i in range(1, 4):
        pl.semaphore_signal(barrier, 1, device_id=aside(i)[1], device_id_type=MESH)

    copies[0].wait()

    def all_to_all(src, dst, send_sem, recv_sem):
        def one(i, _):
            other, device = member(i)
            pltpu.make_async_remote_copy(
                src.at[other], dst.at[g], send_sem, recv_sem, device_id=device, device_id_type=MESH
            ).start()
            return 0

        lax.fori_loop(1, GROUP, one, 0)
        dst[g] = src[g]

    def wait_blocks(ref, count, sem):
        block = ref.at[pl.ds(0, count)]
        pltpu.make_async_copy(block, block, sem).wait()

    for a in range(2):
        for c in range(4):
            copies[1 + a * 4 + c].wait()
            rows = pl.ds(c * chunk, chunk)
            xm[rows, :] = jnp.dot(rows_in[a, rows, :], fx[...], preferred_element_type=F32)

        def turn(y8, _):
            pieces = [
                xm[pl.ds(z * 16 + y2 * 8 + y8, 16, stride=64), :]
                for y2 in range(2)
                for z in range(4)
            ]
            t32[pl.ds(y8, 128, stride=8), :] = jnp.concatenate(pieces, axis=0).T
            return 0

        lax.fori_loop(0, 8, turn, 0)
        send1[a] = t32[...].astype(BF16).reshape(GROUP, 32, 128)
        if a == 0:
            pl.semaphore_wait(barrier, GROUP - 1 + 1 + 3)
        all_to_all(send1.at[a], recv1.at[a], s1_send.at[a], s1_recv.at[a])

    wt_copy.wait()

    def spread(i, _):
        both = wt[i].astype(F32)
        turned = halves_swapped(both)
        low = low_lanes(both.shape)
        w1[i] = jnp.where(low, both, turned)
        w2[i] = jnp.where(low, turned, both)
        return 0

    lax.fori_loop(0, 16, spread, 0)
    fy_copy.wait()

    to_partner = []
    for a in range(2):
        wait_blocks(recv1.at[a], GROUP - 1, s1_recv.at[a])
        for h in range(2):
            block = recv1[a, :, h * 16 : (h + 1) * 16, :].reshape(GROUP * 16, 128)
            both = lax.dot_general(
                block, fy[...], (((0,), (0,)), ((), ())), preferred_element_type=F32
            )
            part[a, h] = both[:64, :128] + both[64:, 128:]
        copy = pltpu.make_async_remote_copy(
            part.at[a, 1 - half], part_in.at[a], px_send.at[a], px_recv.at[a],
            device_id=partner, device_id_type=MESH,
        )
        copy.start()
        to_partner.append(copy)

    low = low_lanes((64, 128))

    to_partner[0].wait_recv()
    spectra = (part[0, half] + part_in[0]).astype(BF16).astype(F32)
    turned = halves_swapped(spectra)
    s_rows[0] = spectra
    s_rows[1] = jnp.where(low, -turned, turned)
    a1[...] = jnp.where(low, spectra, turned)
    a2[...] = jnp.where(low, turned, spectra)
    for z in range(4):

        def mix(i, total):
            return (
                total
                + w1[i] * s_rows[0, pl.ds(z * 16 + i, 1), :]
                + w2[i] * s_rows[1, pl.ds(z * 16 + i, 1), :]
            )

        total = lax.fori_loop(0, 16, mix, jnp.zeros((64, 128), F32))
        mixpart[:, z] = total.reshape(4, 16, 128)
    for i in range(1, 4):
        other, device = aside(i)
        pltpu.make_async_remote_copy(
            mixpart.at[other], mix_in.at[i - 1], rs_send, rs_recv, device_id=device, device_id_type=MESH
        ).start()

    to_partner[1].wait_recv()
    cots[n] = ((part[1, half] + part_in[1]) * 8.0).astype(BF16).reshape(4, 16, 128)
    for i in range(1, 4):
        other, device = aside(i)
        pltpu.make_async_remote_copy(
            cots.at[n], cots.at[n], ag_send, ag_recv, device_id=device, device_id_type=MESH
        ).start()

    back = []

    def to_half(a):
        copy = pltpu.make_async_remote_copy(
            modes.at[a, half], modes.at[a, half], mx_send.at[a], mx_recv.at[a],
            device_id=partner, device_id_type=MESH,
        )
        copy.start()
        back.append(copy)

    wait_blocks(mix_in, 3, rs_recv)
    mixed = mixpart[n] + mix_in[0] + mix_in[1] + mix_in[2]
    modes[0, half] = mixed.astype(BF16).reshape(64, 128)
    to_half(0)

    wait_blocks(cots, 3, ag_recv)
    for o in range(4):
        for z in range(4):
            d = cots[o, z].astype(F32)
            turned = halves_swapped(d)
            d1[z, o * 16 : (o + 1) * 16, :] = d
            d2[z, o * 16 : (o + 1) * 16, :] = jnp.where(low_lanes((16, 128)), turned, -turned)

    def gradient(i, _):
        for z in range(4):
            sums = jnp.sum(w1[i] * d1[z] + w2[i] * d2[z], axis=0, keepdims=True)
            sg[pl.ds(z * 16 + i, 1), :] = sums
        return 0

    lax.fori_loop(0, 16, gradient, 0)
    modes[1, half] = (sg[...] * 0.125).astype(BF16)
    to_half(1)

    for a in range(2):
        back[a].wait_recv()
        for h in range(2):
            m = modes[a, h]
            zero = jnp.zeros_like(m)
            wide = jnp.concatenate(
                [jnp.concatenate([m, zero], axis=1), jnp.concatenate([zero, m], axis=1)], axis=0
            )
            rows = lax.dot_general(
                fy[...], wide, (((1,), (1,)), ((), ())), preferred_element_type=F32
            )
            send2[a, :, h * 16 : (h + 1) * 16, :] = rows.astype(BF16).reshape(GROUP, 16, 128)
        all_to_all(send2.at[a], recv2.at[a], s2_send.at[a], s2_recv.at[a])

    def weight_gradient(i, _):
        total = jnp.zeros((64, 128), F32)
        for z in range(4):
            row = pl.ds(z * 16 + i, 1)
            total += a1[row, :] * d1[z] + a2[row, :] * d2[z]
        wg[i] = total
        return 0

    lax.fori_loop(0, 16, weight_gradient, 0)
    wg_copy = pltpu.make_async_copy(wg, wg_out, wg_sem)
    wg_copy.start()

    for a, out in enumerate((back_out, grad_out)):
        wait_blocks(recv2.at[a], GROUP - 1, s2_recv.at[a])
        t32[...] = recv2[a].reshape(ROWS, 128).astype(F32)

        def turn_back(y8, _):
            block = t32[pl.ds(y8, 128, stride=8), :].T
            for y2 in range(2):
                for z in range(4):
                    at = (y2 * 4 + z) * 16
                    xm[pl.ds(z * 16 + y2 * 8 + y8, 16, stride=64), :] = block[at : at + 16]
            return 0

        lax.fori_loop(0, 8, turn_back, 0)
        out[...] = xm[...].astype(BF16)

    wg_copy.wait()
    for a in range(2):
        wait_blocks(send1.at[a], GROUP - 1, s1_send.at[a])
        wait_blocks(send2.at[a], GROUP - 1, s2_send.at[a])
        to_partner[a].wait_send()
        back[a].wait_send()
    wait_blocks(mix_in, 3, rs_send)
    wait_blocks(cots, 3, ag_send)


def exchange(field, cot, weight, fx, fy):
    any_spec = pl.BlockSpec(memory_space=pl.ANY)
    vmem = pl.BlockSpec(memory_space=pltpu.VMEM)
    dma = pltpu.SemaphoreType.DMA
    return pl.pallas_call(
        exchange_kernel,
        out_shape=(
            jax.ShapeDtypeStruct((ROWS, 128), BF16),
            jax.ShapeDtypeStruct((ROWS, 128), BF16),
            jax.ShapeDtypeStruct((16, 64, 128), F32),
        ),
        in_specs=[any_spec] * 5,
        out_specs=(vmem, vmem, any_spec),
        scratch_shapes=[
            pltpu.VMEM((2, ROWS, X), BF16),
            pltpu.VMEM((X, 128), BF16),
            pltpu.VMEM((GROUP * 16, 256), BF16),
            pltpu.VMEM((16, 64, 128), BF16),
            pltpu.VMEM((16, 64, 128), F32),
            pltpu.VMEM((16, 64, 128), F32),
            pltpu.VMEM((ROWS, 128), F32),
            pltpu.VMEM((ROWS, 128), F32),
            pltpu.VMEM((2, GROUP, 32, 128), BF16),
            pltpu.VMEM((2, GROUP, 32, 128), BF16),
            pltpu.VMEM((2, 2, 64, 128), F32),
            pltpu.VMEM((2, 64, 128), F32),
            pltpu.VMEM((2, 64, 128), F32),
            pltpu.VMEM((64, 128), F32),
            pltpu.VMEM((64, 128), F32),
            pltpu.VMEM((4, 4, 16, 128), F32),
            pltpu.VMEM((3, 4, 16, 128), F32),
            pltpu.VMEM((4, 4, 16, 128), BF16),
            pltpu.VMEM((4, 64, 128), F32),
            pltpu.VMEM((4, 64, 128), F32),
            pltpu.VMEM((64, 128), F32),
            pltpu.VMEM((2, 2, 64, 128), BF16),
            pltpu.VMEM((2, GROUP, 32, 128), BF16),
            pltpu.VMEM((2, GROUP, 32, 128), BF16),
            pltpu.VMEM((16, 64, 128), F32),
            dma((11,)),
            dma((2,)),
            dma((2,)),
            dma((2,)),
            dma((2,)),
            dma,
            dma,
            dma,
            dma,
            dma((2,)),
            dma((2,)),
            dma((2,)),
            dma((2,)),
            dma,
        ],
        compiler_params=pltpu.CompilerParams(
            collective_id=0, has_side_effects=True, vmem_limit_bytes=40 << 20
        ),
    )(field, cot, weight, fx, fy)


def rows_kernel(back, grad, ix, out, fgrad, buf, sem):
    chunk = ROWS // 4
    copies = []
    for a, (src, dst) in enumerate(((back, out), (grad, fgrad))):
        for c in range(4):
            rows = pl.ds(c * chunk, chunk)
            buf[a, rows, :] = jnp.dot(
                src[rows, :], ix[...], preferred_element_type=F32
            ).astype(BF16)
            copy = pltpu.make_async_copy(buf.at[a, rows], dst.at[rows], sem.at[a * 4 + c])
            copy.start()
            copies.append(copy)
    for copy in copies:
        copy.wait()


def rows_back(back, grad, ix):
    any_spec = pl.BlockSpec(memory_space=pl.ANY)
    vmem = pl.BlockSpec(memory_space=pltpu.VMEM)
    return pl.pallas_call(
        rows_kernel,
        out_shape=(jax.ShapeDtypeStruct((ROWS, X), BF16),) * 2,
        in_specs=[vmem] * 3,
        out_specs=(any_spec, any_spec),
        scratch_shapes=[pltpu.VMEM((2, ROWS, X), BF16), pltpu.SemaphoreType.DMA((8,))],
        compiler_params=pltpu.CompilerParams(vmem_limit_bytes=24 << 20),
    )(back, grad, ix)


def solution(mesh):
    forward_x, inverse_x, forward_y = tables()

    def body(field, spectral_weight, cotangent):
        shape = field.shape
        back, grad, weight_grad = exchange(
            field.reshape(ROWS, X),
            cotangent.reshape(ROWS, X),
            spectral_weight.reshape(16, 64, 128),
            jnp.asarray(forward_x),
            jnp.asarray(forward_y),
        )
        output, field_grad = rows_back(back, grad, jnp.asarray(inverse_x))
        return (
            output.reshape(shape),
            weight_grad.reshape(16, 64, 1, 128),
            field_grad.reshape(shape),
        )

    spec = P("narrow", None, "wide", None)
    return jax.shard_map(
        body, mesh=mesh, in_specs=(spec,) * 3, out_specs=(spec,) * 3, check_vma=False
    )
```

profile of v0, /device:TPU:1, one launch (start us, length us, event | category | flops | bytes accessed | tf_op | source)
XLA Modules:
  0.0 51.7 jit_solution(15964049869200869870)
XLA Ops:
  0.6 0.0 copy-start
  0.6 1.6 %copy-done = bf16[16,4,16,1024]{3,2,1,0:T(8,128)(2,1)S(1)} copy-done((bf16[16,4,16,1024]{3,2,1,0:T(8,128)(2,1)S(1)}, bf16[16,4,16,1024]{3,2,1,0:T(8,128)(2,1)}, u32[]{:S(2)}) %copy-start) | copy-done | bytes 2097176
  2.2 0.0 copy-start.1
  2.2 1.6 %copy-done.1 = bf16[16,4,16,1024]{3,2,1,0:T(8,128)(2,1)S(1)} copy-done((bf16[16,4,16,1024]{3,2,1,0:T(8,128)(2,1)S(1)}, bf16[16,4,16,1024]{3,2,1,0:T(8,128)(2,1)}, u32[]{:S(2)}) %copy-start.1) | copy-done | bytes 2097176
  3.8 0.0 copy-start.2
  3.8 1.0 %copy-done.2 = bf16[2,512,256]{2,1,0:T(8,128)(2,1)S(1)} copy-done((bf16[2,512,256]{2,1,0:T(8,128)(2,1)S(1)}, bf16[2,512,256]{2,1,0:T(8,128)(2,1)}, u32[]{:S(2)}) %copy-start.2) | copy-done | bytes 524312
  4.9 0.0 copy-start.3
  4.9 0.9 %copy-done.3 = bf16[16,64,1,128]{3,1,2,0:T(8,128)(2,1)S(1)} copy-done((bf16[16,64,1,128]{3,1,2,0:T(8,128)(2,1)S(1)}, bf16[16,64,1,128]{3,1,2,0:T(8,128)(2,1)}, u32[]{:S(2)}) %copy-start.3) | copy-done | bytes 262168
  5.8 0.0 copy-start.5
  5.8 0.9 %copy-done.5 = bf16[1024,128]{1,0:T(8,128)(2,1)S(1)} copy-done((bf16[1024,128]{1,0:T(8,128)(2,1)S(1)}, bf16[1024,128]{1,0:T(8,128)(2,1)}, u32[]{:S(2)}) %copy-start.5) | copy-done | bytes 262168
  6.8 0.0 copy-start.4
  6.8 41.8 %shard_map.85 = (bf16[1024,128]{1,0:T(8,128)(2,1)S(1)}, bf16[1024,128]{1,0:T(8,128)(2,1)S(1)}, f32[16,64,128]{2,1,0:T(8,128)S(1)}) custom-call(bf16[1024,1024]{1,0:T(8,128)(2,1)S(1)} %bitcast.8, bf16[1024,1024]{1,0:T(8,128)(2,1)S(1)} %bitcast.9, bf16[16,64,128]{2,1,0:T(8,128)(2,1)S(1)} %bitcast.11, bf16[1024,128]{1,0:T(8,128)(2,1)S(1)} %copy-done.5, ...), custom_call_target="tpu_custom_call" | custom-call | tf_op jit(solution)/shard_map/pallas_call | solution.py:296
  48.5 0.0 copy-done.4
  48.6 2.4 %shard_map.86 = (bf16[1024,1024]{1,0:T(8,128)(2,1)}, bf16[1024,1024]{1,0:T(8,128)(2,1)}) custom-call(bf16[1024,128]{1,0:T(8,128)(2,1)S(1)} %get-tuple-element.8.back, bf16[1024,128]{1,0:T(8,128)(2,1)S(1)} %get-tuple-element.9.grad, bf16[128,1024]{1,0:T(8,128)(2,1)S(1)} %copy-done.4), custom_call_target="tpu_custom_call" | custom-call | tf_op jit(solution)/shard_map/pallas_call | solution.py:371
  50.9 0.8 %copy.11 = f32[16,64,1,128]{3,2,1,0:T(1,128)} copy(f32[16,64,1,128]{3,2,1,0:T(1,128)S(1)} %bitcast.10) | data formatting | bytes 1048576
Async XLA Ops:
  0.6 1.6 %copy-start = (bf16[16,4,16,1024]{3,2,1,0:T(8,128)(2,1)S(1)}, bf16[16,4,16,1024]{3,2,1,0:T(8,128)(2,1)}, u32[]{:S(2)}) copy-start(bf16[16,4,16,1024]{3,2,1,0:T(8,128)(2,1)} %param.6) | copy-start | bytes 6291460
  2.2 1.6 %copy-start.1 = (bf16[16,4,16,1024]{3,2,1,0:T(8,128)(2,1)S(1)}, bf16[16,4,16,1024]{3,2,1,0:T(8,128)(2,1)}, u32[]{:S(2)}) copy-start(bf16[16,4,16,1024]{3,2,1,0:T(8,128)(2,1)} %param.8) | copy-start | bytes 6291460
  3.8 1.0 %copy-start.2 = (bf16[2,512,256]{2,1,0:T(8,128)(2,1)S(1)}, bf16[2,512,256]{2,1,0:T(8,128)(2,1)}, u32[]{:S(2)}) copy-start(bf16[2,512,256]{2,1,0:T(8,128)(2,1)} %constant.7.clone.fy_hbm) | copy-start | bytes 1572868
  4.9 0.9 %copy-start.3 = (bf16[16,64,1,128]{3,1,2,0:T(8,128)(2,1)S(1)}, bf16[16,64,1,128]{3,1,2,0:T(8,128)(2,1)}, u32[]{:S(2)}) copy-start(bf16[16,64,1,128]{3,1,2,0:T(8,128)(2,1)} %param.7) | copy-start | bytes 786436
  5.8 0.9 %copy-start.5 = (bf16[1024,128]{1,0:T(8,128)(2,1)S(1)}, bf16[1024,128]{1,0:T(8,128)(2,1)}, u32[]{:S(2)}) copy-start(bf16[1024,128]{1,0:T(8,128)(2,1)} %constant.6.clone.fx_hbm) | copy-start | bytes 786436
  6.8 41.8 %copy-start.4 = (bf16[128,1024]{1,0:T(8,128)(2,1)S(1)}, bf16[128,1024]{1,0:T(8,128)(2,1)}, u32[]{:S(2)}) copy-start(bf16[128,1024]{1,0:T(8,128)(2,1)} %constant.8.clone.ix) | copy-start | bytes 786436
where the time goes:
time: 52 us; the launch traced here: 51.7 us
  Pallas kernels  44.1 us (85%)
  local copies, waits for them, and re-layouts  6.91 us (13%)
  between operations  0.67 us (1%)
    pallas_call x1, Pallas kernels, exchange(): pl.pallas_call(exchange_kernel, out_shape=(jax.ShapeDtypeStruct((ROWS, 12...  41.8 us
    unnamed x13, local copies, waits for them, and re-layouts  6.91 us
    pallas_call x1, Pallas kernels, rows_back(): pl.pallas_call(rows_kernel, out_shape=(jax.ShapeDtypeStruct((ROWS, X), BF...  2.35 us

commit v1 on v0

--- a/solution.py
+++ b/solution.py
@@ -136,7 +136,7 @@
             t32[pl.ds(y8, 128, stride=8), :] = jnp.concatenate(pieces, axis=0).T
             return 0
 
-        lax.fori_loop(0, 8, turn, 0)
+        lax.fori_loop(0, 8, turn, 0, unroll=True)
         send1[a] = t32[...].astype(BF16).reshape(GROUP, 32, 128)
         if a == 0:
             pl.semaphore_wait(barrier, GROUP - 1 + 1 + 3)
@@ -152,11 +152,12 @@
         w2[i] = jnp.where(low, turned, both)
         return 0
 
-    lax.fori_loop(0, 16, spread, 0)
+    lax.fori_loop(0, 16, spread, 0, unroll=2)
     fy_copy.wait()
 
-    to_partner = []
-    for a in range(2):
+    low = low_lanes((64, 128))
+
+    def sums_over_y(a):
         wait_blocks(recv1.at[a], GROUP - 1, s1_recv.at[a])
         for h in range(2):
             block = recv1[a, :, h * 16 : (h + 1) * 16, :].reshape(GROUP * 16, 128)
@@ -169,35 +170,52 @@
             device_id=partner, device_id_type=MESH,
         )
         copy.start()
-        to_partner.append(copy)
-
-    low = low_lanes((64, 128))
-
-    to_partner[0].wait_recv()
+        return copy
+
+    def to_half(a):
+        copy = pltpu.make_async_remote_copy(
+            modes.at[a, half], modes.at[a, half], mx_send.at[a], mx_recv.at[a],
+            device_id=partner, device_id_type=MESH,
+        )
+        copy.start()
+        return copy
+
+    field_part = sums_over_y(0)
+    field_part.wait_recv()
     spectra = (part[0, half] + part_in[0]).astype(BF16).astype(F32)
     turned = halves_swapped(spectra)
     s_rows[0] = spectra
     s_rows[1] = jnp.where(low, -turned, turned)
     a1[...] = jnp.where(low, spectra, turned)
     a2[...] = jnp.where(low, turned, spectra)
-    for z in range(4):
-
-        def mix(i, total):
-            return (
+    for o in range(2):
+
+        def mix(i, totals):
+            x1, x2 = w1[i, o * 32 : (o + 1) * 32, :], w2[i, o * 32 : (o + 1) * 32, :]
+            return tuple(
                 total
-                + w1[i] * s_rows[0, pl.ds(z * 16 + i, 1), :]
-                + w2[i] * s_rows[1, pl.ds(z * 16 + i, 1), :]
+                + x1 * s_rows[0, pl.ds(z * 16 + i, 1), :]
+                + x2 * s_rows[1, pl.ds(z * 16 + i, 1), :]
+                for z, total in enumerate(totals)
             )
 
-        total = lax.fori_loop(0, 16, mix, jnp.zeros((64, 128), F32))
-        mixpart[:, z] = total.reshape(4, 16, 128)
+        totals = lax.fori_loop(0, 16, mix, (jnp.zeros((32, 128), F32),) * 4, unroll=4)
+        for z, total in enumerate(totals):
+            mixpart[o * 2 : (o + 1) * 2, z] = total.reshape(2, 16, 128)
     for i in range(1, 4):
         other, device = aside(i)
         pltpu.make_async_remote_copy(
             mixpart.at[other], mix_in.at[i - 1], rs_send, rs_recv, device_id=device, device_id_type=MESH
         ).start()
 
-    to_partner[1].wait_recv()
+    cot_part = sums_over_y(1)
+
+    wait_blocks(mix_in, 3, rs_recv)
+    mixed = mixpart[n] + mix_in[0] + mix_in[1] + mix_in[2]
+    modes[0, half] = mixed.astype(BF16).reshape(64, 128)
+    field_back = to_half(0)
+
+    cot_part.wait_recv()
     cots[n] = ((part[1, half] + part_in[1]) * 8.0).astype(BF16).reshape(4, 16, 128)
     for i in range(1, 4):
         other, device = aside(i)
@@ -205,41 +223,8 @@
             cots.at[n], cots.at[n], ag_send, ag_recv, device_id=device, device_id_type=MESH
         ).start()
 
-    back = []
-
-    def to_half(a):
-        copy = pltpu.make_async_remote_copy(
-            modes.at[a, half], modes.at[a, half], mx_send.at[a], mx_recv.at[a],
-            device_id=partner, device_id_type=MESH,
-        )
-        copy.start()
-        back.append(copy)
-
-    wait_blocks(mix_in, 3, rs_recv)
-    mixed = mixpart[n] + mix_in[0] + mix_in[1] + mix_in[2]
-    modes[0, half] = mixed.astype(BF16).reshape(64, 128)
-    to_half(0)
-
-    wait_blocks(cots, 3, ag_recv)
-    for o in range(4):
-        for z in range(4):
-            d = cots[o, z].astype(F32)
-            turned = halves_swapped(d)
-            d1[z, o * 16 : (o + 1) * 16, :] = d
-            d2[z, o * 16 : (o + 1) * 16, :] = jnp.where(low_lanes((16, 128)), turned, -turned)
-
-    def gradient(i, _):
-        for z in range(4):
-            sums = jnp.sum(w1[i] * d1[z] + w2[i] * d2[z], axis=0, keepdims=True)
-            sg[pl.ds(z * 16 + i, 1), :] = sums
-        return 0
-
-    lax.fori_loop(0, 16, gradient, 0)
-    modes[1, half] = (sg[...] * 0.125).astype(BF16)
-    to_half(1)
-
-    for a in range(2):
-        back[a].wait_recv()
+    def rows_of_y(a, copy):
+        copy.wait_recv()
         for h in range(2):
             m = modes[a, h]
             zero = jnp.zeros_like(m)
@@ -252,15 +237,38 @@
             send2[a, :, h * 16 : (h + 1) * 16, :] = rows.astype(BF16).reshape(GROUP, 16, 128)
         all_to_all(send2.at[a], recv2.at[a], s2_send.at[a], s2_recv.at[a])
 
+    rows_of_y(0, field_back)
+
+    wait_blocks(cots, 3, ag_recv)
+    for o in range(4):
+        for z in range(4):
+            d = cots[o, z].astype(F32)
+            turned = halves_swapped(d)
+            d1[z, o * 16 : (o + 1) * 16, :] = d
+            d2[z, o * 16 : (o + 1) * 16, :] = jnp.where(low_lanes((16, 128)), turned, -turned)
+
+    def gradient(i, _):
+        x1, x2 = w1[i], w2[i]
+        for z in range(4):
+            sg[pl.ds(z * 16 + i, 1), :] = jnp.sum(x1 * d1[z] + x2 * d2[z], axis=0, keepdims=True)
+        return 0
+
+    lax.fori_loop(0, 16, gradient, 0, unroll=2)
+    modes[1, half] = (sg[...] * 0.125).astype(BF16)
+    cot_back = to_half(1)
+    rows_of_y(1, cot_back)
+
     def weight_gradient(i, _):
-        total = jnp.zeros((64, 128), F32)
-        for z in range(4):
-            row = pl.ds(z * 16 + i, 1)
-            total += a1[row, :] * d1[z] + a2[row, :] * d2[z]
-        wg[i] = total
+        for o in range(2):
+            total = jnp.zeros((32, 128), F32)
+            for z in range(4):
+                row = pl.ds(z * 16 + i, 1)
+                outs = slice(o * 32, (o + 1) * 32)
+                total += a1[row, :] * d1[z, outs, :] + a2[row, :] * d2[z, outs, :]
+            wg[i, o * 32 : (o + 1) * 32, :] = total
         return 0
 
-    lax.fori_loop(0, 16, weight_gradient, 0)
+    lax.fori_loop(0, 16, weight_gradient, 0, unroll=2)
     wg_copy = pltpu.make_async_copy(wg, wg_out, wg_sem)
     wg_copy.start()
 
@@ -276,21 +284,21 @@
                     xm[pl.ds(z * 16 + y2 * 8 + y8, 16, stride=64), :] = block[at : at + 16]
             return 0
 
-        lax.fori_loop(0, 8, turn_back, 0)
+        lax.fori_loop(0, 8, turn_back, 0, unroll=True)
         out[...] = xm[...].astype(BF16)
 
-    wg_copy.wait()
-    for a in range(2):
+    for a, (first, second) in enumerate(((field_part, field_back), (cot_part, cot_back))):
         wait_blocks(send1.at[a], GROUP - 1, s1_send.at[a])
         wait_blocks(send2.at[a], GROUP - 1, s2_send.at[a])
-        to_partner[a].wait_send()
-        back[a].wait_send()
+        first.wait_send()
+        second.wait_send()
+    wg_copy.wait()
     wait_blocks(mix_in, 3, rs_send)
     wait_blocks(cots, 3, ag_send)
 
 
 def exchange(field, cot, weight, fx, fy):
-    any_spec = pl.BlockSpec(memory_space=pl.ANY)
+    hbm = pl.BlockSpec(memory_space=pltpu.HBM)
     vmem = pl.BlockSpec(memory_space=pltpu.VMEM)
     dma = pltpu.SemaphoreType.DMA
     return pl.pallas_call(
@@ -300,8 +308,8 @@
             jax.ShapeDtypeStruct((ROWS, 128), BF16),
             jax.ShapeDtypeStruct((16, 64, 128), F32),
         ),
-        in_specs=[any_spec] * 5,
-        out_specs=(vmem, vmem, any_spec),
+        in_specs=[hbm] * 5,
+        out_specs=(vmem, vmem, hbm),
         scratch_shapes=[
             pltpu.VMEM((2, ROWS, X), BF16),
             pltpu.VMEM((X, 128), BF16),
@@ -342,16 +350,17 @@
             dma((2,)),
             dma((2,)),
             dma,
-        ],
+            ],
         compiler_params=pltpu.CompilerParams(
-            collective_id=0, has_side_effects=True, vmem_limit_bytes=40 << 20
+            collective_id=0, has_side_effects=True, vmem_limit_bytes=55836672
         ),
     )(field, cot, weight, fx, fy)
 
 
-def rows_kernel(back, grad, ix, out, fgrad, buf, sem):
+def rows_kernel(back, grad, wg, ix, out, wg_out, fgrad, buf, sem):
     chunk = ROWS // 4
-    copies = []
+    copies = [pltpu.make_async_copy(wg, wg_out, sem.at[8])]
+    copies[0].start()
     for a, (src, dst) in enumerate(((back, out), (grad, fgrad))):
         for c in range(4):
             rows = pl.ds(c * chunk, chunk)
@@ -365,17 +374,18 @@
         copy.wait()
 
 
-def rows_back(back, grad, ix):
-    any_spec = pl.BlockSpec(memory_space=pl.ANY)
+def rows_back(back, grad, wg, ix):
+    hbm = pl.BlockSpec(memory_space=pltpu.HBM)
     vmem = pl.BlockSpec(memory_space=pltpu.VMEM)
+    rows = jax.ShapeDtypeStruct((ROWS, X), BF16)
     return pl.pallas_call(
         rows_kernel,
-        out_shape=(jax.ShapeDtypeStruct((ROWS, X), BF16),) * 2,
-        in_specs=[vmem] * 3,
-        out_specs=(any_spec, any_spec),
-        scratch_shapes=[pltpu.VMEM((2, ROWS, X), BF16), pltpu.SemaphoreType.DMA((8,))],
-        compiler_params=pltpu.CompilerParams(vmem_limit_bytes=24 << 20),
-    )(back, grad, ix)
+        out_shape=(rows, jax.ShapeDtypeStruct((ROWS, 128), F32), rows),
+        in_specs=[vmem, vmem, hbm, vmem],
+        out_specs=(hbm,) * 3,
+        scratch_shapes=[pltpu.VMEM((2, ROWS, X), BF16), pltpu.SemaphoreType.DMA((9,))],
+        compiler_params=pltpu.CompilerParams(vmem_limit_bytes=55574528),
+    )(back, grad, wg, ix)
 
 
 def solution(mesh):
@@ -390,7 +400,9 @@
             jnp.asarray(forward_x),
             jnp.asarray(forward_y),
         )
-        output, field_grad = rows_back(back, grad, jnp.asarray(inverse_x))
+        output, weight_grad, field_grad = rows_back(
+            back, grad, weight_grad.reshape(ROWS, 128), jnp.asarray(inverse_x)
+        )
         return (
             output.reshape(shape),
             weight_grad.reshape(16, 64, 1, 128),

time: 52 us -> 64.2 us (1.23)
  Pallas kernels: 44.1 us -> 63.4 us
  local copies, waits for them, and re-layouts: 6.91 us -> 0.01 us
    pallas_call x1, Pallas kernels: 2.35 us -> 17.1 us  [rows_back(): pl.pallas_call(rows_kernel, out_shape=(rows, jax.ShapeDtypeStruct((ROWS,...]
    unnamed x13 -> x2, local copies, waits for them, and re-layouts: 6.91 us -> 0.01 us
    pallas_call x1, Pallas kernels: 41.8 us -> 46.4 us  [exchange(): pl.pallas_call(exchange_kernel, out_shape=(jax.ShapeDtypeStruct((ROWS, 12...]
where the time goes in v1:
time: 64.2 us; the launch traced here: 64.1 us
  Pallas kernels  63.4 us (99%)
  between operations  0.65 us (1%)
    pallas_call x1, Pallas kernels, exchange(): pl.pallas_call(exchange_kernel, out_shape=(jax.ShapeDtypeStruct((ROWS, 12...  46.4 us
    pallas_call x1, Pallas kernels, rows_back(): pl.pallas_call(rows_kernel, out_shape=(rows, jax.ShapeDtypeStruct((ROWS,...  17.1 us

profile of v1, /device:TPU:1, one launch (start us, length us, event | category | flops | bytes accessed | tf_op | source)
XLA Modules:
  0.0 64.1 jit_solution(10371310639066445674)
XLA Ops:
  0.6 0.0 copy-start
  0.6 46.4 %shard_map.85 = (bf16[1024,128]{1,0:T(8,128)(2,1)S(1)}, bf16[1024,128]{1,0:T(8,128)(2,1)S(1)}, f32[16,64,128]{2,1,0:T(8,128)}) custom-call(bf16[1024,1024]{1,0:T(8,128)(2,1)} %bitcast.9, bf16[1024,1024]{1,0:T(8,128)(2,1)} %bitcast.10, bf16[16,64,128]{2,1,0:T(8,128)(2,1)} %bitcast.12, bf16[1024,128]{1,0:T(8,128)(2,1)} %constant.6.clone.fx_hbm, ...), custom_call_target="tpu_custom_call" | custom-call | tf_op jit(solution)/shard_map/pallas_call | solution.py:304
  47.0 0.0 copy-done
  47.0 17.1 %shard_map.86 = (bf16[1024,1024]{1,0:T(8,128)(2,1)}, f32[1024,128]{1,0:T(8,128)}, bf16[1024,1024]{1,0:T(8,128)(2,1)}) custom-call(bf16[1024,128]{1,0:T(8,128)(2,1)S(1)} %get-tuple-element.9.back, bf16[1024,128]{1,0:T(8,128)(2,1)S(1)} %get-tuple-element.10.grad, f32[1024,128]{1,0:T(8,128)} %bitcast.11, bf16[128,1024]{1,0:T(8,128)(2,1)S(1)} %copy-done), custom_call_target="tpu_custom_call" | custom-call | tf_op jit(solution)/shard_map/pallas_call | solution.py:381
Async XLA Ops:
  0.6 46.4 %copy-start = (bf16[128,1024]{1,0:T(8,128)(2,1)S(1)}, bf16[128,1024]{1,0:T(8,128)(2,1)}, u32[]{:S(2)}) copy-start(bf16[128,1024]{1,0:T(8,128)(2,1)} %constant.8.clone.ix) | copy-start | bytes 786436

commit v2 on v0

v2 whole, which is shorter than its diff:
```python
import math

import jax
import jax.numpy as jnp
import ml_dtypes
import numpy as np
from jax import lax
from jax.experimental import pallas as pl
from jax.experimental.pallas import tpu as pltpu
from jax.sharding import PartitionSpec as P

X = 1024
Y = 1024
MX = 64
MY = 64
GROUP = 32
ROWS = 1024
MESH = pl.DeviceIdType.MESH
F32 = jnp.float32
BF16 = jnp.bfloat16


def mode_of(group, half):
    return (group // 2) * 4 + half * 2 + group % 2


def tables():
    step = np.float32(2.0 * math.pi / X)
    group = np.arange(GROUP)
    k = np.stack([mode_of(group, h) for h in range(2)], axis=1)
    ax = ((np.arange(X)[:, None, None] * k[None]) % X).astype(np.float32) * step
    fx = np.stack([np.cos(ax), -np.sin(ax)], axis=-1).reshape(X, 2 * MX)
    forward_x = (fx / np.float32(32)).astype(ml_dtypes.bfloat16)
    inverse_x = np.ascontiguousarray((fx / np.float32(4)).astype(ml_dtypes.bfloat16).T)
    m = np.arange(MY)
    q = np.where(m < MY // 2, m, m - MY + Y)
    ay = ((np.arange(Y)[:, None] * q[None]) % Y).astype(np.float32) * step
    cos, sin = np.cos(ay), np.sin(ay)
    fy = np.stack([np.concatenate([cos, -sin], 1), np.concatenate([sin, cos], 1)], 0)
    fy = (fy / np.float32(32)).astype(ml_dtypes.bfloat16)
    halves = []
    for h in range(2):
        y = 16 * mode_of(group, h)[:, None] + np.arange(16)[None]
        part = fy[:, y, :].reshape(2, GROUP, 2, 8, 2 * MY)
        halves.append(part.transpose(1, 0, 3, 2, 4).reshape(GROUP * 16, 4 * MY))
    return forward_x, inverse_x, np.stack(halves)


def halves_swapped(a):
    return pltpu.roll(a, MY, a.ndim - 1)


def low_lanes(shape):
    return lax.broadcasted_iota(jnp.int32, shape, len(shape) - 1) < MY


def spread_cots(cots, d1, d2):
    for o in range(4):
        for z in range(4):
            d = cots[o, z].astype(F32)
            turned = halves_swapped(d)
            d1[z, o * 16 : (o + 1) * 16, :] = d
            d2[z, o * 16 : (o + 1) * 16, :] = jnp.where(low_lanes((16, 128)), turned, -turned)


def far_first():
    offsets = [(dy, dx, dc) for dy in range(4) for dx in range(4) for dc in range(2)]
    return sorted(offsets[1:], key=lambda o: -(min(o[0], 4 - o[0]) + min(o[1], 4 - o[1])))


RING = (4, 3, 5, 2, 6, 1, 7)
COT, FIELD = 0, 1


def exchange_kernel(
    cot, field, weight, fx_hbm, fy_hbm,
    grad_out, back_out, spectra_out, cots,
    rows_in, fx, fy, wt, w1, w2, xm, t32, send1, recv1, part, part_f32, part_in, s_rows,
    mixpart, mix_in, cots_in, d1, d2, sg, modes, send2, recv2,
    in_sem, s1_send, s1_recv, px_send, px_recv, mix_send, mix_recv, cots_send, cots_recv,
    mx_send, mx_recv, s2_send, s2_recv,
):
    w = lax.axis_index("wide")
    n = lax.axis_index("narrow")
    at_y, at_x, half, core = lax.div(w, 16), lax.rem(lax.div(w, 4), 4), lax.rem(lax.div(w, 2), 2), lax.rem(w, 2)
    g = lax.div(w, 4) * 2 + core
    at_z = half * 4 + n
    partner = {"wide": w + 2 - 4 * half, "narrow": n}

    def member(offset):
        dy, dx, dc = offset
        chip = lax.rem(at_y + dy, 4) * 4 + lax.rem(at_x + dx, 4)
        to_core = lax.rem(core + dc, 2)
        return chip * 2 + to_core, {"wide": chip * 4 + half * 2 + to_core, "narrow": n}

    def along_z(offset):
        z = lax.rem(at_z + offset, 8)
        to_half, to_n = lax.div(z, 4), lax.rem(z, 4)
        return to_half, to_n, {"wide": w + 2 * (to_half - half), "narrow": to_n}

    chunk = ROWS // 4
    copies = []
    copies.append(pltpu.make_async_copy(fx_hbm, fx, in_sem.at[8]))
    for a, src in enumerate((cot, field)):
        for c in range(4):
            rows = pl.ds(c * chunk, chunk)
            copies.append(
                pltpu.make_async_copy(src.at[rows], rows_in.at[a, rows], in_sem.at[a * 4 + c])
            )
    fy_copy = pltpu.make_async_copy(fy_hbm.at[half], fy, in_sem.at[9])
    wt_copy = pltpu.make_async_copy(weight, wt, in_sem.at[10])
    for copy in copies:
        copy.start()
    fy_copy.start()
    wt_copy.start()

    barrier = pltpu.get_barrier_semaphore()
    for offset in far_first():
        pl.semaphore_signal(barrier, 1, device_id=member(offset)[1], device_id_type=MESH)
    for offset in RING:
        pl.semaphore_signal(barrier, 1, device_id=along_z(offset)[2], device_id_type=MESH)

    copies[0].wait()

    def all_to_all(src, dst, send_sem, recv_sem):
        for offset in far_first():
            other, device = member(offset)
            pltpu.make_async_remote_copy(
                src.at[other], dst.at[g], send_sem, recv_sem, device_id=device, device_id_type=MESH
            ).start()
        dst[g] = src[g]

    def wait_blocks(ref, count, sem):
        block = ref.at[pl.ds(0, count)]
        pltpu.make_async_copy(block, block, sem).wait()

    def x_transform(a):
        for c in range(4):
            copies[1 + a * 4 + c].wait()
            rows = pl.ds(c * chunk, chunk)
            xm[a, rows, :] = jnp.dot(rows_in[a, rows, :], fx[...], preferred_element_type=F32)

    def blocks_for_modes(a):
        def turn(y8, _):
            pieces = [
                xm[a, pl.ds(z * 16 + y2 * 8 + y8, 16, stride=64), :]
                for y2 in range(2)
                for z in range(4)
            ]
            t32[pl.ds(y8, 128, stride=8), :] = jnp.concatenate(pieces, axis=0).T
            return 0

        lax.fori_loop(0, 8, turn, 0, unroll=True)
        send1[a] = t32[...].astype(BF16).reshape(GROUP, 32, 128)

    x_transform(COT)
    blocks_for_modes(COT)
    x_transform(FIELD)
    pl.semaphore_wait(barrier, GROUP - 1 + 7)
    all_to_all(send1.at[COT], recv1.at[COT], s1_send.at[COT], s1_recv.at[COT])
    blocks_for_modes(FIELD)
    all_to_all(send1.at[FIELD], recv1.at[FIELD], s1_send.at[FIELD], s1_recv.at[FIELD])

    wt_copy.wait()

    def spread(i, _):
        both = wt[i].astype(F32)
        turned = halves_swapped(both)
        low = low_lanes(both.shape)
        w1[i] = jnp.where(low, both, turned)
        w2[i] = jnp.where(low, turned, both)
        return 0

    lax.fori_loop(0, 16, spread, 0, unroll=2)
    fy_copy.wait()

    def sums_over_y(a):
        wait_blocks(recv1.at[a], GROUP - 1, s1_recv.at[a])
        for h in range(2):
            block = recv1[a, :, h * 16 : (h + 1) * 16, :].reshape(GROUP * 16, 128)
            both = lax.dot_general(
                block, fy[...], (((0,), (0,)), ((), ())), preferred_element_type=F32
            )
            sums = both[:64, :128] + both[64:, 128:]
            if a == FIELD:
                part_f32[h] = sums
            part[a, h] = sums.astype(BF16)

    sums_over_y(COT)
    for offset in RING:
        to_half, _, device = along_z(offset)
        pltpu.make_async_remote_copy(
            part.at[COT, to_half], cots_in.at[at_z], cots_send, cots_recv, device_id=device, device_id_type=MESH
        ).start()
    cots_in[at_z] = part[COT, half]

    sums_over_y(FIELD)
    field_part = pltpu.make_async_remote_copy(
        part.at[FIELD, 1 - half], part_in, px_send, px_recv, device_id=partner, device_id_type=MESH
    )
    field_part.start()

    wait_blocks(cots_in, 7, cots_recv)
    for o in range(4):
        both = cots_in[o].astype(F32) + cots_in[4 + o].astype(F32)
        cots[o] = (both * 8.0).astype(BF16).reshape(4, 16, 128)
    spread_cots(cots, d1, d2)

    def gradient(i, _):
        x1, x2 = w1[i], w2[i]
        for z in range(4):
            sg[pl.ds(z * 16 + i, 1), :] = jnp.sum(x1 * d1[z] + x2 * d2[z], axis=0, keepdims=True)
        return 0

    lax.fori_loop(0, 16, gradient, 0, unroll=2)
    modes[COT, half] = (sg[...] * 0.125).astype(BF16)
    cot_back = pltpu.make_async_remote_copy(
        modes.at[COT, half], modes.at[COT, half], mx_send, mx_recv, device_id=partner, device_id_type=MESH
    )
    cot_back.start()

    field_part.wait_recv()
    low = low_lanes((64, 128))
    spectra = (part_f32[half] + part_in[...].astype(F32)).astype(BF16).astype(F32)
    turned = halves_swapped(spectra)
    s_rows[0] = spectra
    s_rows[1] = jnp.where(low, -turned, turned)
    spectra_out[...] = spectra
    for o in range(2):

        def mix(i, totals):
            x1, x2 = w1[i, o * 32 : (o + 1) * 32, :], w2[i, o * 32 : (o + 1) * 32, :]
            return tuple(
                total
                + x1 * s_rows[0, pl.ds(z * 16 + i, 1), :]
                + x2 * s_rows[1, pl.ds(z * 16 + i, 1), :]
                for z, total in enumerate(totals)
            )

        totals = lax.fori_loop(0, 16, mix, (jnp.zeros((32, 128), F32),) * 4, unroll=4)
        for z, total in enumerate(totals):
            for k in range(2):
                mixpart[o * 2 + k, z * 16 : (z + 1) * 16, :] = total[k * 16 : (k + 1) * 16].astype(BF16)
    for offset in RING:
        _, to_n, device = along_z(offset)
        pltpu.make_async_remote_copy(
            mixpart.at[to_n], mix_in.at[at_z], mix_send, mix_recv, device_id=device, device_id_type=MESH
        ).start()
    mix_in[at_z] = mixpart[n]

    def rows_of_y(a):
        for h in range(2):
            m = modes[a, h]
            zero = jnp.zeros_like(m)
            wide = jnp.concatenate(
                [jnp.concatenate([m, zero], axis=1), jnp.concatenate([zero, m], axis=1)], axis=0
            )
            rows = lax.dot_general(
                fy[...], wide, (((1,), (1,)), ((), ())), preferred_element_type=F32
            )
            send2[a, :, h * 16 : (h + 1) * 16, :] = rows.astype(BF16).reshape(GROUP, 16, 128)
        all_to_all(send2.at[a], recv2.at[a], s2_send.at[a], s2_recv.at[a])

    cot_back.wait_recv()
    rows_of_y(COT)

    wait_blocks(mix_in, 7, mix_recv)
    for h in range(2):
        total = mix_in[h * 4].astype(F32)
        for k in range(1, 4):
            total += mix_in[h * 4 + k].astype(F32)
        modes[FIELD, h] = total.astype(BF16)
    rows_of_y(FIELD)

    for a, out in ((COT, grad_out), (FIELD, back_out)):
        wait_blocks(recv2.at[a], GROUP - 1, s2_recv.at[a])
        t32[...] = recv2[a].reshape(ROWS, 128).astype(F32)

        def turn_back(y8, _):
            block = t32[pl.ds(y8, 128, stride=8), :].T
            for y2 in range(2):
                for z in range(4):
                    at = (y2 * 4 + z) * 16
                    xm[a, pl.ds(z * 16 + y2 * 8 + y8, 16, stride=64), :] = block[at : at + 16]
            return 0

        lax.fori_loop(0, 8, turn_back, 0, unroll=True)
        out[...] = xm[a].astype(BF16)

    for a in range(2):
        wait_blocks(send1.at[a], GROUP - 1, s1_send.at[a])
        wait_blocks(send2.at[a], GROUP - 1, s2_send.at[a])
    field_part.wait_send()
    cot_back.wait_send()
    wait_blocks(cots_in, 7, cots_send)
    wait_blocks(mix_in, 7, mix_send)


def exchange(cot, field, weight, fx, fy):
    hbm = pl.BlockSpec(memory_space=pltpu.HBM)
    vmem = pl.BlockSpec(memory_space=pltpu.VMEM)
    dma = pltpu.SemaphoreType.DMA
    return pl.pallas_call(
        exchange_kernel,
        out_shape=(
            jax.ShapeDtypeStruct((ROWS, 128), BF16),
            jax.ShapeDtypeStruct((ROWS, 128), BF16),
            jax.ShapeDtypeStruct((64, 128), F32),
            jax.ShapeDtypeStruct((4, 4, 16, 128), BF16),
        ),
        in_specs=[hbm] * 5,
        out_specs=(vmem,) * 4,
        scratch_shapes=[
            pltpu.VMEM((2, ROWS, X), BF16),
            pltpu.VMEM((X, 128), BF16),
            pltpu.VMEM((GROUP * 16, 256), BF16),
            pltpu.VMEM((16, 64, 128), BF16),
            pltpu.VMEM((16, 64, 128), F32),
            pltpu.VMEM((16, 64, 128), F32),
            pltpu.VMEM((2, ROWS, 128), F32),
            pltpu.VMEM((ROWS, 128), F32),
            pltpu.VMEM((2, GROUP, 32, 128), BF16),
            pltpu.VMEM((2, GROUP, 32, 128), BF16),
            pltpu.VMEM((2, 2, 64, 128), BF16),
            pltpu.VMEM((2, 64, 128), F32),
            pltpu.VMEM((64, 128), BF16),
            pltpu.VMEM((2, 64, 128), F32),
            pltpu.VMEM((4, 64, 128), BF16),
            pltpu.VMEM((8, 64, 128), BF16),
            pltpu.VMEM((8, 64, 128), BF16),
            pltpu.VMEM((4, 64, 128), F32),
            pltpu.VMEM((4, 64, 128), F32),
            pltpu.VMEM((64, 128), F32),
            pltpu.VMEM((2, 2, 64, 128), BF16),
            pltpu.VMEM((2, GROUP, 32, 128), BF16),
            pltpu.VMEM((2, GROUP, 32, 128), BF16),
            dma((11,)),
            dma((2,)),
            dma((2,)),
            dma,
            dma,
            dma,
            dma,
            dma,
            dma,
            dma,
            dma,
            dma((2,)),
            dma((2,)),
        ],
        compiler_params=pltpu.CompilerParams(
            collective_id=0, has_side_effects=True, vmem_limit_bytes=55705600
        ),
    )(cot, field, weight, fx, fy)


def rows_kernel(
    back, grad, spectra, cots, ix, out, wg_out, fgrad, buf, a1, a2, d1, d2, wg, sem
):
    chunk = ROWS // 4
    copies = []

    def rows_out(a, src, dst):
        for c in range(4):
            rows = pl.ds(c * chunk, chunk)
            buf[a, rows, :] = jnp.dot(
                src[rows, :], ix[...], preferred_element_type=F32
            ).astype(BF16)
            copy = pltpu.make_async_copy(buf.at[a, rows], dst.at[rows], sem.at[a * 4 + c])
            copy.start()
            copies.append(copy)

    rows_out(0, back, out)

    s = spectra[...]
    turned = halves_swapped(s)
    low = low_lanes((64, 128))
    a1[...] = jnp.where(low, s, turned)
    a2[...] = jnp.where(low, turned, s)
    spread_cots(cots, d1, d2)

    def weight_gradient(i, _):
        for o in range(2):
            total = jnp.zeros((32, 128), F32)
            for z in range(4):
                row = pl.ds(z * 16 + i, 1)
                outs = slice(o * 32, (o + 1) * 32)
                total += a1[row, :] * d1[z, outs, :] + a2[row, :] * d2[z, outs, :]
            wg[pl.ds(pl.multiple_of(i * 64 + o * 32, 32), 32), :] = total
        return 0

    lax.fori_loop(0, 16, weight_gradient, 0, unroll=2)
    copy = pltpu.make_async_copy(wg, wg_out, sem.at[8])
    copy.start()
    copies.append(copy)

    rows_out(1, grad, fgrad)
    for copy in copies:
        copy.wait()


def rows_back(back, grad, spectra, cots, ix):
    hbm = pl.BlockSpec(memory_space=pltpu.HBM)
    vmem = pl.BlockSpec(memory_space=pltpu.VMEM)
    rows = jax.ShapeDtypeStruct((ROWS, X), BF16)
    return pl.pallas_call(
        rows_kernel,
        out_shape=(rows, jax.ShapeDtypeStruct((ROWS, 128), F32), rows),
        in_specs=[vmem] * 5,
        out_specs=(hbm,) * 3,
        scratch_shapes=[
            pltpu.VMEM((2, ROWS, X), BF16),
            pltpu.VMEM((64, 128), F32),
            pltpu.VMEM((64, 128), F32),
            pltpu.VMEM((4, 64, 128), F32),
            pltpu.VMEM((4, 64, 128), F32),
            pltpu.VMEM((ROWS, 128), F32),
            pltpu.SemaphoreType.DMA((9,)),
        ],
        compiler_params=pltpu.CompilerParams(vmem_limit_bytes=55443456),
    )(back, grad, spectra, cots, ix)


def solution(mesh):
    forward_x, inverse_x, forward_y = tables()

    def body(field, spectral_weight, cotangent):
        shape = field.shape
        grad, back, spectra, cots = exchange(
            cotangent.reshape(ROWS, X),
            field.reshape(ROWS, X),
            spectral_weight.reshape(16, 64, 128),
            jnp.asarray(forward_x),
            jnp.asarray(forward_y),
        )
        output, weight_grad, field_grad = rows_back(
            back, grad, spectra, cots, jnp.asarray(inverse_x)
        )
        return (
            output.reshape(shape),
            weight_grad.reshape(16, 64, 1, 128),
            field_grad.reshape(shape),
        )

    spec = P("narrow", None, "wide", None)
    return jax.shard_map(
        body, mesh=mesh, in_specs=(spec,) * 3, out_specs=(spec,) * 3, check_vma=False
    )
```

time: 52 us -> 40.9 us (0.79)
  local copies, waits for them, and re-layouts: 6.91 us -> 0.01 us
  Pallas kernels: 44.1 us -> 40.1 us
    unnamed x13 -> x2, local copies, waits for them, and re-layouts: 6.91 us -> 0.01 us
    pallas_call x1, Pallas kernels: 41.8 us -> 37.5 us  [exchange(): pl.pallas_call(exchange_kernel, out_shape=(jax.ShapeDtypeStruct((ROWS, 12...]
where the time goes in v2:
time: 40.9 us; the launch traced here: 40.8 us
  Pallas kernels  40.1 us (98%)
  between operations  0.65 us (2%)
    pallas_call x1, Pallas kernels, exchange(): pl.pallas_call(exchange_kernel, out_shape=(jax.ShapeDtypeStruct((ROWS, 12...  37.5 us
    pallas_call x1, Pallas kernels, rows_back(): pl.pallas_call(rows_kernel, out_shape=(rows, jax.ShapeDtypeStruct((ROWS,...  2.68 us

profile of v2, /device:TPU:1, one launch (start us, length us, event | category | flops | bytes accessed | tf_op | source)
XLA Modules:
  0.0 40.8 jit_solution(5142760021107562513)
XLA Ops:
  0.6 0.0 copy-start
  0.6 37.5 %shard_map.85 = (bf16[1024,128]{1,0:T(8,128)(2,1)S(1)}, bf16[1024,128]{1,0:T(8,128)(2,1)S(1)}, f32[64,128]{1,0:T(8,128)S(1)}, bf16[4,4,16,128]{3,2,1,0:T(8,128)(2,1)S(1)}) custom-call(bf16[1024,1024]{1,0:T(8,128)(2,1)} %bitcast.8, bf16[1024,1024]{1,0:T(8,128)(2,1)} %bitcast.9, bf16[16,64,128]{2,1,0:T(8,128)(2,1)} %bitcast.10, ...), custom_call_target="tpu_custom_call" | custom-call | tf_op jit(solution)/shard_map/pallas_call | solution.py:303
  38.1 0.0 copy-done
  38.1 2.7 %shard_map.86 = (bf16[1024,1024]{1,0:T(8,128)(2,1)}, f32[1024,128]{1,0:T(8,128)}, bf16[1024,1024]{1,0:T(8,128)(2,1)}) custom-call(bf16[1024,128]{1,0:T(8,128)(2,1)S(1)} %get-tuple-element.10.back, bf16[1024,128]{1,0:T(8,128)(2,1)S(1)} %get-tuple-element.11.grad, f32[64,128]{1,0:T(8,128)S(1)} %get-tuple-element.12.spectra, ...), custom_call_target="tpu_custom_call" | custom-call | tf_op jit(solution)/shard_map/pallas_call | solution.py:406
Async XLA Ops:
  0.6 37.5 %copy-start = (bf16[128,1024]{1,0:T(8,128)(2,1)S(1)}, bf16[128,1024]{1,0:T(8,128)(2,1)}, u32[]{:S(2)}) copy-start(bf16[128,1024]{1,0:T(8,128)(2,1)} %constant.8.clone.ix) | copy-start | bytes 786436

commit v3 on v2

v3 whole, which is shorter than its diff:
```python
import math

import jax
import jax.numpy as jnp
import ml_dtypes
import numpy as np
from jax import lax
from jax.experimental import pallas as pl
from jax.experimental.pallas import tpu as pltpu
from jax.sharding import PartitionSpec as P

X = 1024
Y = 1024
MX = 64
MY = 64
GROUP = 32
ROWS = 1024
MESH = pl.DeviceIdType.MESH
F32 = jnp.float32
BF16 = jnp.bfloat16


def mode_of(group, half):
    return (group // 2) * 4 + half * 2 + group % 2


def tables():
    step = np.float32(2.0 * math.pi / X)
    group = np.arange(GROUP)
    k = np.stack([mode_of(group, h) for h in range(2)], axis=1)
    ax = ((np.arange(X)[:, None, None] * k[None]) % X).astype(np.float32) * step
    fx = np.stack([np.cos(ax), -np.sin(ax)], axis=-1).reshape(X, 2 * MX)
    forward_x = (fx / np.float32(32)).astype(ml_dtypes.bfloat16)
    inverse_x = np.ascontiguousarray((fx / np.float32(4)).astype(ml_dtypes.bfloat16).T)
    m = np.arange(MY)
    q = np.where(m < MY // 2, m, m - MY + Y)
    ay = ((np.arange(Y)[:, None] * q[None]) % Y).astype(np.float32) * step
    cos, sin = np.cos(ay), np.sin(ay)
    fy = np.stack([np.concatenate([cos, -sin], 1), np.concatenate([sin, cos], 1)], 0)
    fy = (fy / np.float32(32)).astype(ml_dtypes.bfloat16)
    halves = []
    for h in range(2):
        y = 16 * mode_of(group, h)[:, None] + np.arange(16)[None]
        part = fy[:, y, :].reshape(2, GROUP, 2, 8, 2 * MY)
        halves.append(part.transpose(1, 0, 3, 2, 4).reshape(GROUP * 16, 4 * MY))
    return forward_x, inverse_x, np.stack(halves)


def halves_swapped(a):
    return pltpu.roll(a, MY, a.ndim - 1)


def low_lanes(shape):
    return lax.broadcasted_iota(jnp.int32, shape, len(shape) - 1) < MY


def far_first():
    offsets = [(dy, dx, dc) for dy in range(4) for dx in range(4) for dc in range(2)]
    return sorted(offsets[1:], key=lambda o: -(min(o[0], 4 - o[0]) + min(o[1], 4 - o[1])))


COT, FIELD = 0, 1
FAR, OWN = 0, 1


def exchange_kernel(
    cot, field, weight, fx_hbm, fy_hbm,
    grad_out, back_out, wg,
    rows_in, fx, fy, wt, w1, w2, xm, t32, send1, recv1, part, part_own, part_in, s_rows,
    a1, a2, mixpart, mix_in, cots_in, d1, d2, sg, modes, send2, recv2,
    in_sem, s1_send, s1_recv, px_send, px_recv, mix_send, mix_recv, cots_send, cots_recv,
    mx_send, mx_recv, s2_send, s2_recv,
):
    w = lax.axis_index("wide")
    n = lax.axis_index("narrow")
    at_y, at_x, half, core = lax.div(w, 16), lax.rem(lax.div(w, 4), 4), lax.rem(lax.div(w, 2), 2), lax.rem(w, 2)
    g = lax.div(w, 4) * 2 + core
    at_z = half * 4 + n
    partner = {"wide": w + 2 - 4 * half, "narrow": n}

    def member(offset):
        dy, dx, dc = offset
        chip = lax.rem(at_y + dy, 4) * 4 + lax.rem(at_x + dx, 4)
        to_core = lax.rem(core + dc, 2)
        return chip * 2 + to_core, {"wide": chip * 4 + half * 2 + to_core, "narrow": n}

    modes_of = (1 - half, half)

    def along_z(r):
        wide = w + 2 * (modes_of[r] - half)
        for i in (0, 1, 3, 2) if r == FAR else (2, 1, 3):
            to_n = lax.rem(n + i, 4)
            yield to_n, {"wide": wide, "narrow": to_n}

    chunk = ROWS // 4
    copies = []
    copies.append(pltpu.make_async_copy(fx_hbm, fx, in_sem.at[8]))
    for a, src in enumerate((cot, field)):
        for c in range(4):
            rows = pl.ds(c * chunk, chunk)
            copies.append(
                pltpu.make_async_copy(src.at[rows], rows_in.at[a, rows], in_sem.at[a * 4 + c])
            )
    fy_copy = pltpu.make_async_copy(fy_hbm.at[half], fy, in_sem.at[9])
    wt_copy = pltpu.make_async_copy(weight, wt, in_sem.at[10])
    for copy in copies:
        copy.start()
    fy_copy.start()
    wt_copy.start()

    barrier = pltpu.get_barrier_semaphore()
    for offset in far_first():
        pl.semaphore_signal(barrier, 1, device_id=member(offset)[1], device_id_type=MESH)
    for r in (FAR, OWN):
        for _, device in along_z(r):
            pl.semaphore_signal(barrier, 1, device_id=device, device_id_type=MESH)

    copies[0].wait()

    def all_to_all(a, r, sent, received, send_sem, recv_sem):
        src, dst = sent.at[a, modes_of[r]], received.at[a, modes_of[r]]
        for offset in far_first():
            other, device = member(offset)
            pltpu.make_async_remote_copy(
                src.at[other], dst.at[g], send_sem.at[a, r], recv_sem.at[a, r],
                device_id=device, device_id_type=MESH,
            ).start()
        dst[g] = src[g]

    def wait_blocks(ref, count, sem):
        block = ref.at[pl.ds(0, count)]
        pltpu.make_async_copy(block, block, sem).wait()

    def x_transform(a):
        for c in range(4):
            copies[1 + a * 4 + c].wait()
            rows = pl.ds(c * chunk, chunk)
            xm[a, rows, :] = jnp.dot(rows_in[a, rows, :], fx[...], preferred_element_type=F32)

    def blocks_for_modes(a):
        def turn(y8, _):
            pieces = [
                xm[a, pl.ds(z * 16 + y2 * 8 + y8, 16, stride=64), :]
                for y2 in range(2)
                for z in range(4)
            ]
            t32[pl.ds(y8, 128, stride=8), :] = jnp.concatenate(pieces, axis=0).T
            return 0

        lax.fori_loop(0, 8, turn, 0, unroll=True)
        blocks = t32[...].astype(BF16).reshape(GROUP, 2, 16, 128)
        for h in range(2):
            send1[a, h] = blocks[:, h]

    x_transform(COT)
    blocks_for_modes(COT)
    x_transform(FIELD)
    pl.semaphore_wait(barrier, GROUP - 1 + 7)
    all_to_all(COT, FAR, send1, recv1, s1_send, s1_recv)
    blocks_for_modes(FIELD)
    all_to_all(FIELD, FAR, send1, recv1, s1_send, s1_recv)
    all_to_all(COT, OWN, send1, recv1, s1_send, s1_recv)
    all_to_all(FIELD, OWN, send1, recv1, s1_send, s1_recv)

    wt_copy.wait()

    def spread(i, _):
        both = wt[i].astype(F32)
        turned = halves_swapped(both)
        low = low_lanes(both.shape)
        w1[i] = jnp.where(low, both, turned)
        w2[i] = jnp.where(low, turned, both)
        return 0

    lax.fori_loop(0, 16, spread, 0, unroll=2)
    fy_copy.wait()

    def sums_over_y(a, r):
        wait_blocks(recv1.at[a, 0], GROUP - 1, s1_recv.at[a, r])
        block = recv1[a, modes_of[r]].reshape(GROUP * 16, 128)
        both = lax.dot_general(
            block, fy[...], (((0,), (0,)), ((), ())), preferred_element_type=F32
        )
        return both[:64, :128] + both[64:, 128:]

    def cots_along_z(r):
        part[COT, r] = sums_over_y(COT, r).astype(BF16)
        for _, device in along_z(r):
            pltpu.make_async_remote_copy(
                part.at[COT, r], cots_in.at[at_z], cots_send.at[r], cots_recv.at[r],
                device_id=device, device_id_type=MESH,
            ).start()

    cots_along_z(FAR)

    part[FIELD, FAR] = sums_over_y(FIELD, FAR).astype(BF16)
    field_part = pltpu.make_async_remote_copy(
        part.at[FIELD, FAR], part_in, px_send, px_recv, device_id=partner, device_id_type=MESH
    )
    field_part.start()

    cots_along_z(OWN)
    cots_in[at_z] = part[COT, OWN]
    part_own[...] = sums_over_y(FIELD, OWN)

    field_part.wait_recv()
    low = low_lanes((64, 128))
    spectra = (part_own[...] + part_in[...].astype(F32)).astype(BF16).astype(F32)
    turned = halves_swapped(spectra)
    s_rows[0] = spectra
    s_rows[1] = jnp.where(low, -turned, turned)
    a1[...] = jnp.where(low, spectra, turned)
    a2[...] = jnp.where(low, turned, spectra)
    for o in range(2):

        def mix(i, totals):
            x1, x2 = w1[i, o * 32 : (o + 1) * 32, :], w2[i, o * 32 : (o + 1) * 32, :]
            return tuple(
                total
                + x1 * s_rows[0, pl.ds(z * 16 + i, 1), :]
                + x2 * s_rows[1, pl.ds(z * 16 + i, 1), :]
                for z, total in enumerate(totals)
            )

        totals = lax.fori_loop(0, 16, mix, (jnp.zeros((32, 128), F32),) * 4, unroll=4)
        for z, total in enumerate(totals):
            for k in range(2):
                mixpart[o * 2 + k, z * 16 : (z + 1) * 16, :] = total[k * 16 : (k + 1) * 16].astype(BF16)
    for r in (OWN, FAR):
        for to_n, device in along_z(r):
            pltpu.make_async_remote_copy(
                mixpart.at[to_n], mix_in.at[at_z], mix_send.at[r], mix_recv.at[r],
                device_id=device, device_id_type=MESH,
            ).start()
    mix_in[at_z] = mixpart[n]

    wait_blocks(cots_in, 4, cots_recv.at[FAR])
    wait_blocks(cots_in, 3, cots_recv.at[OWN])
    low = low_lanes((64, 128))
    for o in range(4):
        both = cots_in[o].astype(F32) + cots_in[4 + o].astype(F32)
        rounded = (both * 8.0).astype(BF16)
        d = rounded.astype(F32)
        turned = halves_swapped(d)
        d1[:, o * 16 : (o + 1) * 16, :] = d.reshape(4, 16, 128)
        d2[:, o * 16 : (o + 1) * 16, :] = jnp.where(low, turned, -turned).reshape(4, 16, 128)

    def gradient(i, _):
        x1, x2 = w1[i], w2[i]
        for z in range(4):
            terms = (x1 * d1[z] + x2 * d2[z]).reshape(8, 8, 128)
            sg[pl.ds(pl.multiple_of((z * 16 + i) * 8, 8), 8), :] = jnp.sum(terms, axis=0)
        return 0

    lax.fori_loop(0, 16, gradient, 0, unroll=4)
    sums = sg[pl.ds(0, 64, stride=8), :]
    for k in range(1, 8):
        sums += sg[pl.ds(k, 64, stride=8), :]
    modes[COT, half] = (sums * 0.125).astype(BF16)
    cot_back = pltpu.make_async_remote_copy(
        modes.at[COT, half], modes.at[COT, half], mx_send, mx_recv, device_id=partner, device_id_type=MESH
    )
    cot_back.start()

    def rows_of_y(a, r):
        m = modes[a, modes_of[r]]
        zero = jnp.zeros_like(m)
        wide = jnp.concatenate(
            [jnp.concatenate([m, zero], axis=1), jnp.concatenate([zero, m], axis=1)], axis=0
        )
        rows = lax.dot_general(fy[...], wide, (((1,), (1,)), ((), ())), preferred_element_type=F32)
        send2[a, modes_of[r]] = rows.astype(BF16).reshape(GROUP, 16, 128)
        all_to_all(a, r, send2, recv2, s2_send, s2_recv)

    def mixed_rows(r):
        wait_blocks(mix_in, 4 if r == FAR else 3, mix_recv.at[r])
        first = modes_of[r] * 4
        total = mix_in[first].astype(F32)
        for k in range(1, 4):
            total += mix_in[first + k].astype(F32)
        modes[FIELD, modes_of[r]] = total.astype(BF16)
        rows_of_y(FIELD, r)

    rows_of_y(COT, OWN)

    mixed_rows(OWN)
    cot_back.wait_recv()
    rows_of_y(COT, FAR)
    mixed_rows(FAR)

    def weight_gradient(i, _):
        for o in range(2):
            total = jnp.zeros((32, 128), F32)
            for z in range(4):
                row = pl.ds(z * 16 + i, 1)
                outs = slice(o * 32, (o + 1) * 32)
                total += a1[row, :] * d1[z, outs, :] + a2[row, :] * d2[z, outs, :]
            wg[pl.ds(pl.multiple_of(i * 64 + o * 32, 32), 32), :] = total
        return 0

    lax.fori_loop(0, 16, weight_gradient, 0, unroll=2)

    for a, out in ((COT, grad_out), (FIELD, back_out)):
        blocks = t32.reshape(GROUP, 2, 16, 128)
        for r in range(2):
            wait_blocks(recv2.at[a, 0], GROUP - 1, s2_recv.at[a, r])
        for h in range(2):
            blocks[:, h] = recv2[a, h].astype(F32)

        def turn_back(y8, _):
            block = t32[pl.ds(y8, 128, stride=8), :].T
            for y2 in range(2):
                for z in range(4):
                    at = (y2 * 4 + z) * 16
                    xm[a, pl.ds(z * 16 + y2 * 8 + y8, 16, stride=64), :] = block[at : at + 16]
            return 0

        lax.fori_loop(0, 8, turn_back, 0, unroll=True)
        out[...] = xm[a].astype(BF16)

    for a in range(2):
        for r in range(2):
            wait_blocks(send1.at[a, 0], GROUP - 1, s1_send.at[a, r])
            wait_blocks(send2.at[a, 0], GROUP - 1, s2_send.at[a, r])
    field_part.wait_send()
    cot_back.wait_send()
    for r, count in ((FAR, 4), (OWN, 3)):
        wait_blocks(cots_in, count, cots_send.at[r])
        wait_blocks(mix_in, count, mix_send.at[r])


def exchange(cot, field, weight, fx, fy):
    hbm = pl.BlockSpec(memory_space=pltpu.HBM)
    vmem = pl.BlockSpec(memory_space=pltpu.VMEM)
    dma = pltpu.SemaphoreType.DMA
    return pl.pallas_call(
        exchange_kernel,
        out_shape=(
            pltpu.VMEM((ROWS, 128), BF16),
            pltpu.VMEM((ROWS, 128), BF16),
            pltpu.VMEM((ROWS, 128), F32),
        ),
        in_specs=[hbm] * 5,
        out_specs=(vmem,) * 3,
        scratch_shapes=[
            pltpu.VMEM((2, ROWS, X), BF16),
            pltpu.VMEM((X, 128), BF16),
            pltpu.VMEM((GROUP * 16, 256), BF16),
            pltpu.VMEM((16, 64, 128), BF16),
            pltpu.VMEM((16, 64, 128), F32),
            pltpu.VMEM((16, 64, 128), F32),
            pltpu.VMEM((2, ROWS, 128), F32),
            pltpu.VMEM((ROWS, 128), F32),
            pltpu.VMEM((2, 2, GROUP, 16, 128), BF16),
            pltpu.VMEM((2, 2, GROUP, 16, 128), BF16),
            pltpu.VMEM((2, 2, 64, 128), BF16),
            pltpu.VMEM((64, 128), F32),
            pltpu.VMEM((64, 128), BF16),
            pltpu.VMEM((2, 64, 128), F32),
            pltpu.VMEM((64, 128), F32),
            pltpu.VMEM((64, 128), F32),
            pltpu.VMEM((4, 64, 128), BF16),
            pltpu.VMEM((8, 64, 128), BF16),
            pltpu.VMEM((8, 64, 128), BF16),
            pltpu.VMEM((4, 64, 128), F32),
            pltpu.VMEM((4, 64, 128), F32),
            pltpu.VMEM((512, 128), F32),
            pltpu.VMEM((2, 2, 64, 128), BF16),
            pltpu.VMEM((2, 2, GROUP, 16, 128), BF16),
            pltpu.VMEM((2, 2, GROUP, 16, 128), BF16),
            dma((11,)),
            dma((2, 2)),
            dma((2, 2)),
            dma,
            dma,
            dma((2,)),
            dma((2,)),
            dma((2,)),
            dma((2,)),
            dma,
            dma,
            dma((2, 2)),
            dma((2, 2)),
        ],
        compiler_params=pltpu.CompilerParams(
            collective_id=0, has_side_effects=True, vmem_limit_bytes=44 << 20
        ),
    )(*(pltpu.with_memory_space_constraint(a, pltpu.HBM) for a in (cot, field, weight, fx, fy)))


def rows_kernel(grad, back, wg, ix, fgrad, wg_out, out, buf, sem):
    chunk = ROWS // 4
    copies = [pltpu.make_async_copy(wg, wg_out, sem.at[8])]
    copies[0].start()
    for a, (src, dst) in enumerate(((grad, fgrad), (back, out))):
        for c in range(4):
            rows = pl.ds(c * chunk, chunk)
            buf[a, rows, :] = jnp.dot(
                src[rows, :], ix[...], preferred_element_type=F32
            ).astype(BF16)
            copy = pltpu.make_async_copy(buf.at[a, rows], dst.at[rows], sem.at[a * 4 + c])
            copy.start()
            copies.append(copy)
    for copy in copies:
        copy.wait()


def rows_back(grad, back, wg, ix):
    hbm = pl.BlockSpec(memory_space=pltpu.HBM)
    vmem = pl.BlockSpec(memory_space=pltpu.VMEM)
    rows = jax.ShapeDtypeStruct((ROWS, X), BF16)
    return pl.pallas_call(
        rows_kernel,
        out_shape=(rows, jax.ShapeDtypeStruct((ROWS, 128), F32), rows),
        in_specs=[vmem] * 4,
        out_specs=(hbm,) * 3,
        scratch_shapes=[
            pltpu.VMEM((2, ROWS, X), BF16),
            pltpu.SemaphoreType.DMA((9,)),
        ],
        compiler_params=pltpu.CompilerParams(vmem_limit_bytes=44 << 20),
    )(grad, back, wg, ix)


def solution(mesh):
    forward_x, inverse_x, forward_y = tables()

    def body(field, spectral_weight, cotangent):
        shape = field.shape
        grad, back, weight_grad = exchange(
            cotangent.reshape(ROWS, X),
            field.reshape(ROWS, X),
            spectral_weight.reshape(16, 64, 128),
            jnp.asarray(forward_x),
            jnp.asarray(forward_y),
        )
        field_grad, weight_grad, output = rows_back(
            grad, back, weight_grad, jnp.asarray(inverse_x)
        )
        return (
            output.reshape(shape),
            weight_grad.reshape(16, 64, 1, 128),
            field_grad.reshape(shape),
        )

    spec = P("narrow", None, "wide", None)
    return jax.shard_map(
        body, mesh=mesh, in_specs=(spec,) * 3, out_specs=(spec,) * 3, check_vma=False
    )
```

time: 40.9 us -> 39.3 us (0.961)
  Pallas kernels: 40.1 us -> 38.5 us
    pallas_call x1, Pallas kernels: 37.5 us -> 36.2 us  [exchange(): pl.pallas_call(exchange_kernel, out_shape=(pltpu.VMEM((ROWS, 128), BF16),...]
where the time goes in v3:
time: 39.3 us; the launch traced here: 39.2 us
  Pallas kernels  38.5 us (98%)
  between operations  0.65 us (2%)
    pallas_call x1, Pallas kernels, exchange(): pl.pallas_call(exchange_kernel, out_shape=(pltpu.VMEM((ROWS, 128), BF16),...  36.2 us
    pallas_call x1, Pallas kernels, rows_back(): pl.pallas_call(rows_kernel, out_shape=(rows, jax.ShapeDtypeStruct((ROWS,...  2.36 us

profile of v3, /device:TPU:1, one launch (start us, length us, event | category | flops | bytes accessed | tf_op | source)
XLA Modules:
  0.0 39.2 jit_solution(12335109025140230949)
XLA Ops:
  0.6 0.0 copy-start
  0.6 36.2 %shard_map.85 = (bf16[1024,128]{1,0:T(8,128)(2,1)S(1)}, bf16[1024,128]{1,0:T(8,128)(2,1)S(1)}, f32[1024,128]{1,0:T(8,128)S(1)}) custom-call(bf16[1024,1024]{1,0:T(8,128)(2,1)} %bitcast.8, bf16[1024,1024]{1,0:T(8,128)(2,1)} %bitcast.9, bf16[16,64,128]{2,1,0:T(8,128)(2,1)} %bitcast.10, bf16[1024,128]{1,0:T(8,128)(2,1)} %constant.6.clone.fx_hbm, ...), custom_call_target="tpu_custom_call" | custom-call | tf_op jit(solution)/shard_map/pallas_call | solution.py:336
  36.8 0.0 copy-done
  36.8 2.4 %shard_map.86 = (bf16[1024,1024]{1,0:T(8,128)(2,1)}, f32[1024,128]{1,0:T(8,128)}, bf16[1024,1024]{1,0:T(8,128)(2,1)}) custom-call(bf16[1024,128]{1,0:T(8,128)(2,1)S(1)} %get-tuple-element.9.grad, bf16[1024,128]{1,0:T(8,128)(2,1)S(1)} %get-tuple-element.10.back, f32[1024,128]{1,0:T(8,128)S(1)} %get-tuple-element.11.wg, bf16[128,1024]{1,0:T(8,128)(2,1)S(1)} %copy-done), custom_call_target="tpu_custom_call" | custom-call | tf_op jit(solution)/shard_map/pallas_call | solution.py:412
Async XLA Ops:
  0.6 36.2 %copy-start = (bf16[128,1024]{1,0:T(8,128)(2,1)S(1)}, bf16[128,1024]{1,0:T(8,128)(2,1)}, u32[]{:S(2)}) copy-start(bf16[128,1024]{1,0:T(8,128)(2,1)} %constant.8.clone.ix) | copy-start | bytes 786436

commit v4 on v3

--- a/solution.py
+++ b/solution.py
@@ -60,6 +60,24 @@
 
 
 COT, FIELD = 0, 1
+
+
+def rows_from_blocks(blocks, t32, xm):
+    parts = t32.reshape(GROUP, 2, 16, 128)
+    for h in range(2):
+        parts[:, h] = blocks[h].astype(F32)
+
+    def turn_back(y8, _):
+        block = t32[pl.ds(y8, 128, stride=8), :].T
+        for y2 in range(2):
+            for z in range(4):
+                at = (y2 * 4 + z) * 16
+                xm[pl.ds(z * 16 + y2 * 8 + y8, 16, stride=64), :] = block[at : at + 16]
+        return 0
+
+    lax.fori_loop(0, 8, turn_back, 0, unroll=True)
+
+
 FAR, OWN = 0, 1
 
 
@@ -91,6 +109,13 @@
         for i in (0, 1, 3, 2) if r == FAR else (2, 1, 3):
             to_n = lax.rem(n + i, 4)
             yield to_n, {"wide": wide, "narrow": to_n}
+
+    barrier = pltpu.get_barrier_semaphore()
+    for offset in far_first():
+        pl.semaphore_signal(barrier, 1, device_id=member(offset)[1], device_id_type=MESH)
+    for r in (FAR, OWN):
+        for _, device in along_z(r):
+            pl.semaphore_signal(barrier, 1, device_id=device, device_id_type=MESH)
 
     chunk = ROWS // 4
     copies = []
@@ -108,13 +133,6 @@
     fy_copy.start()
     wt_copy.start()
 
-    barrier = pltpu.get_barrier_semaphore()
-    for offset in far_first():
-        pl.semaphore_signal(barrier, 1, device_id=member(offset)[1], device_id_type=MESH)
-    for r in (FAR, OWN):
-        for _, device in along_z(r):
-            pl.semaphore_signal(barrier, 1, device_id=device, device_id_type=MESH)
-
     copies[0].wait()
 
     def all_to_all(a, r, sent, received, send_sem, recv_sem):
@@ -300,23 +318,13 @@
 
     lax.fori_loop(0, 16, weight_gradient, 0, unroll=2)
 
-    for a, out in ((COT, grad_out), (FIELD, back_out)):
-        blocks = t32.reshape(GROUP, 2, 16, 128)
-        for r in range(2):
-            wait_blocks(recv2.at[a, 0], GROUP - 1, s2_recv.at[a, r])
-        for h in range(2):
-            blocks[:, h] = recv2[a, h].astype(F32)
-
-        def turn_back(y8, _):
-            block = t32[pl.ds(y8, 128, stride=8), :].T
-            for y2 in range(2):
-                for z in range(4):
-                    at = (y2 * 4 + z) * 16
-                    xm[a, pl.ds(z * 16 + y2 * 8 + y8, 16, stride=64), :] = block[at : at + 16]
-            return 0
-
-        lax.fori_loop(0, 8, turn_back, 0, unroll=True)
-        out[...] = xm[a].astype(BF16)
+    for r in range(2):
+        wait_blocks(recv2.at[COT, 0], GROUP - 1, s2_recv.at[COT, r])
+    rows_from_blocks(recv2.at[COT], t32, xm.at[COT])
+    grad_out[...] = xm[COT].astype(BF16)
+    for r in range(2):
+        wait_blocks(recv2.at[FIELD, 0], GROUP - 1, s2_recv.at[FIELD, r])
+    back_out[...] = recv2[FIELD]
 
     for a in range(2):
         for r in range(2):
@@ -337,7 +345,7 @@
         exchange_kernel,
         out_shape=(
             pltpu.VMEM((ROWS, 128), BF16),
-            pltpu.VMEM((ROWS, 128), BF16),
+            pltpu.VMEM((2, GROUP, 16, 128), BF16),
             pltpu.VMEM((ROWS, 128), F32),
         ),
         in_specs=[hbm] * 5,
@@ -388,15 +396,17 @@
     )(*(pltpu.with_memory_space_constraint(a, pltpu.HBM) for a in (cot, field, weight, fx, fy)))
 
 
-def rows_kernel(grad, back, wg, ix, fgrad, wg_out, out, buf, sem):
+def rows_kernel(grad, back, wg, ix, fgrad, wg_out, out, buf, t32, xm, sem):
     chunk = ROWS // 4
     copies = [pltpu.make_async_copy(wg, wg_out, sem.at[8])]
     copies[0].start()
-    for a, (src, dst) in enumerate(((grad, fgrad), (back, out))):
+    for a, (src, dst) in enumerate(((grad, fgrad), (xm, out))):
+        if a == FIELD:
+            rows_from_blocks(back, t32, xm)
         for c in range(4):
             rows = pl.ds(c * chunk, chunk)
             buf[a, rows, :] = jnp.dot(
-                src[rows, :], ix[...], preferred_element_type=F32
+                src[rows, :].astype(BF16), ix[...], preferred_element_type=F32
             ).astype(BF16)
             copy = pltpu.make_async_copy(buf.at[a, rows], dst.at[rows], sem.at[a * 4 + c])
             copy.start()
@@ -416,6 +426,8 @@
         out_specs=(hbm,) * 3,
         scratch_shapes=[
             pltpu.VMEM((2, ROWS, X), BF16),
+            pltpu.VMEM((ROWS, 128), F32),
+            pltpu.VMEM((ROWS, 128), F32),
             pltpu.SemaphoreType.DMA((9,)),
         ],
         compiler_params=pltpu.CompilerParams(vmem_limit_bytes=44 << 20),

time: 39.3 us -> 38.6 us (0.982)
  Pallas kernels: 38.5 us -> 37.8 us
    pallas_call x1, Pallas kernels: 36.2 us -> 35.3 us  [exchange(): pl.pallas_call(exchange_kernel, out_shape=(pltpu.VMEM((ROWS, 128), BF16),...]
where the time goes in v4:
time: 38.6 us; the launch traced here: 38.5 us
  Pallas kernels  37.8 us (98%)
  between operations  0.65 us (2%)
    pallas_call x1, Pallas kernels, exchange(): pl.pallas_call(exchange_kernel, out_shape=(pltpu.VMEM((ROWS, 128), BF16),...  35.3 us
    pallas_call x1, Pallas kernels, rows_back(): pl.pallas_call(rows_kernel, out_shape=(rows, jax.ShapeDtypeStruct((ROWS,...  2.58 us

profile of v4, /device:TPU:1, one launch (start us, length us, event | category | flops | bytes accessed | tf_op | source)
XLA Modules:
  0.0 38.5 jit_solution(13498879638808645478)
XLA Ops:
  0.6 0.0 copy-start
  0.6 35.3 %shard_map.85 = (bf16[1024,128]{1,0:T(8,128)(2,1)S(1)}, bf16[2,32,16,128]{3,2,1,0:T(8,128)(2,1)S(1)}, f32[1024,128]{1,0:T(8,128)S(1)}) custom-call(bf16[1024,1024]{1,0:T(8,128)(2,1)} %bitcast.8, bf16[1024,1024]{1,0:T(8,128)(2,1)} %bitcast.9, bf16[16,64,128]{2,1,0:T(8,128)(2,1)} %bitcast.10, bf16[1024,128]{1,0:T(8,128)(2,1)} %constant.6.clone.fx_hbm, ...), custom_call_target="tpu_custom_call" | custom-call | tf_op jit(solution)/shard_map/pallas_call | solution.py:344
  35.9 0.0 copy-done
  35.9 2.6 %shard_map.86 = (bf16[1024,1024]{1,0:T(8,128)(2,1)}, f32[1024,128]{1,0:T(8,128)}, bf16[1024,1024]{1,0:T(8,128)(2,1)}) custom-call(bf16[1024,128]{1,0:T(8,128)(2,1)S(1)} %get-tuple-element.9.grad, bf16[2,32,16,128]{3,2,1,0:T(8,128)(2,1)S(1)} %get-tuple-element.10.back, f32[1024,128]{1,0:T(8,128)S(1)} %get-tuple-element.11.wg, bf16[128,1024]{1,0:T(8,128)(2,1)S(1)} %copy-done), custom_call_target="tpu_custom_call" | custom-call | tf_op jit(solution)/shard_map/pallas_call | solution.py:422
Async XLA Ops:
  0.6 35.3 %copy-start = (bf16[128,1024]{1,0:T(8,128)(2,1)S(1)}, bf16[128,1024]{1,0:T(8,128)(2,1)}, u32[]{:S(2)}) copy-start(bf16[128,1024]{1,0:T(8,128)(2,1)} %constant.8.clone.ix) | copy-start | bytes 786436

commit v5 on v4

--- a/solution.py
+++ b/solution.py
@@ -397,18 +397,18 @@
 
 
 def rows_kernel(grad, back, wg, ix, fgrad, wg_out, out, buf, t32, xm, sem):
-    chunk = ROWS // 4
-    copies = [pltpu.make_async_copy(wg, wg_out, sem.at[8])]
+    chunk = ROWS // 8
+    copies = [pltpu.make_async_copy(wg, wg_out, sem.at[16])]
     copies[0].start()
     for a, (src, dst) in enumerate(((grad, fgrad), (xm, out))):
         if a == FIELD:
             rows_from_blocks(back, t32, xm)
-        for c in range(4):
+        for c in range(8):
             rows = pl.ds(c * chunk, chunk)
             buf[a, rows, :] = jnp.dot(
                 src[rows, :].astype(BF16), ix[...], preferred_element_type=F32
             ).astype(BF16)
-            copy = pltpu.make_async_copy(buf.at[a, rows], dst.at[rows], sem.at[a * 4 + c])
+            copy = pltpu.make_async_copy(buf.at[a, rows], dst.at[rows], sem.at[a * 8 + c])
             copy.start()
             copies.append(copy)
     for copy in copies:
@@ -428,7 +428,7 @@
             pltpu.VMEM((2, ROWS, X), BF16),
             pltpu.VMEM((ROWS, 128), F32),
             pltpu.VMEM((ROWS, 128), F32),
-            pltpu.SemaphoreType.DMA((9,)),
+            pltpu.SemaphoreType.DMA((17,)),
         ],
         compiler_params=pltpu.CompilerParams(vmem_limit_bytes=44 << 20),
     )(grad, back, wg, ix)

time: 38.6 us -> 38.6 us (level)
  no operation moved by 1% of the time
where the time goes in v5:
time: 38.6 us; the launch traced here: 38.5 us
  Pallas kernels  37.8 us (98%)
  between operations  0.65 us (2%)
    pallas_call x1, Pallas kernels, exchange(): pl.pallas_call(exchange_kernel, out_shape=(pltpu.VMEM((ROWS, 128), BF16),...  35.3 us
    pallas_call x1, Pallas kernels, rows_back(): pl.pallas_call(rows_kernel, out_shape=(rows, jax.ShapeDtypeStruct((ROWS,...  2.56 us

profile of v5, /device:TPU:1, one launch (start us, length us, event | category | flops | bytes accessed | tf_op | source)
XLA Modules:
  0.0 38.5 jit_solution(17851876445390892304)
XLA Ops:
  0.6 0.0 copy-start
  0.6 35.3 %shard_map.85 = (bf16[1024,128]{1,0:T(8,128)(2,1)S(1)}, bf16[2,32,16,128]{3,2,1,0:T(8,128)(2,1)S(1)}, f32[1024,128]{1,0:T(8,128)S(1)}) custom-call(bf16[1024,1024]{1,0:T(8,128)(2,1)} %bitcast.8, bf16[1024,1024]{1,0:T(8,128)(2,1)} %bitcast.9, bf16[16,64,128]{2,1,0:T(8,128)(2,1)} %bitcast.10, bf16[1024,128]{1,0:T(8,128)(2,1)} %constant.6.clone.fx_hbm, ...), custom_call_target="tpu_custom_call" | custom-call | tf_op jit(solution)/shard_map/pallas_call | solution.py:344
  35.9 0.0 copy-done
  35.9 2.6 %shard_map.86 = (bf16[1024,1024]{1,0:T(8,128)(2,1)}, f32[1024,128]{1,0:T(8,128)}, bf16[1024,1024]{1,0:T(8,128)(2,1)}) custom-call(bf16[1024,128]{1,0:T(8,128)(2,1)S(1)} %get-tuple-element.9.grad, bf16[2,32,16,128]{3,2,1,0:T(8,128)(2,1)S(1)} %get-tuple-element.10.back, f32[1024,128]{1,0:T(8,128)S(1)} %get-tuple-element.11.wg, bf16[128,1024]{1,0:T(8,128)(2,1)S(1)} %copy-done), custom_call_target="tpu_custom_call" | custom-call | tf_op jit(solution)/shard_map/pallas_call | solution.py:422
Async XLA Ops:
  0.6 35.3 %copy-start = (bf16[128,1024]{1,0:T(8,128)(2,1)S(1)}, bf16[128,1024]{1,0:T(8,128)(2,1)}, u32[]{:S(2)}) copy-start(bf16[128,1024]{1,0:T(8,128)(2,1)} %constant.8.clone.ix) | copy-start | bytes 786436
